TPU v7x, 32 devices: a whole 2x2x4 slice. The times are simulated.
32 devices in a mesh: group: 1, node: 2 (over core), expert: 16 (over z, y, x).
Axes of the slice: x: 2, y: 2, z: 4, core: 2. Of those that a mesh axis runs over, the one named last changes fastest.
Arguments:
- tokens: bfloat16 [512, 7168], P(('group', 'node', 'expert')), may hold values from -6 to 6
- copy_ids: int32 [512, 4], P(('group', 'node', 'expert')), may hold values from 0 to 7, all different within a row; in each aligned block of 16 rows (0 to 15, 16 to 31, ...) at most 16 rows name the same one
- route_weight: float32 [512, 4], P(('group', 'node', 'expert')), may hold values from 0.05 to 1
- placement: int32 [8], replicated, may hold values from 0 to 7, each once
- gate_up: bfloat16 [32, 7168, 512], P(('node', 'expert')), may hold values from -0.0625 to 0.0625
- down_proj: bfloat16 [32, 256, 7168], P(('node', 'expert')), may hold values from -0.1875 to 0.1875
Outputs:
- mixed: bfloat16 [512, 7168], P(('group', 'node', 'expert'))
Inputs may be any that keep to these rules, and one draw needn't show every extreme that they name: `copy_ids`: each token names 4 different copies; among the 16 tokens of one device (aligned blocks of rows) no copy is named more than 16 times, a bound that some block reaches. `placement`: a permutation of the slots.
All inputs are finite; a program needn't handle non-finite values.
Results may differ from a plain program's by a relative error of at most 0.0057.
Values may be sent and summed in bfloat16 or wider, within the bound.
A program may use at most 128 MiB of HBM per device.

v0:
```python
import jax
import jax.numpy as jnp
from jax import lax
from jax.sharding import PartitionSpec as P


def shards(tokens, copy_ids, route_weight, placement, gate_up, down_proj):
    tok_count, top_count = copy_ids.shape
    ffw_piece = down_proj.shape[1]
    model_width = tokens.shape[1]
    slot_total = placement.shape[0]
    devices = lax.axis_size(("node", "expert"))
    shard_count = devices // slot_total
    most_rows = min(tok_count, 2 * tok_count * top_count // slot_total)
    pair_count = tok_count * top_count
    pair_index = jnp.arange(pair_count, dtype=jnp.int32)
    flat_copy = copy_ids.reshape(-1)
    lookup = flat_copy[:, None] == jnp.arange(slot_total, dtype=jnp.int32)[None, :]
    pair_slot = jnp.sum(jnp.where(lookup, placement[None, :], 0), axis=1)
    earlier = (pair_slot[:, None] == pair_slot[None, :]) & (
        pair_index[None, :] < pair_index[:, None]
    )
    ranking = jnp.sum(earlier.astype(jnp.int32), axis=1)
    target = pair_slot * most_rows + ranking
    buffer_rows = slot_total * most_rows
    placing = (jnp.arange(buffer_rows, dtype=jnp.int32)[:, None] == target[None, :]).astype(
        jnp.bfloat16
    )
    owner_map = (
        (pair_index // top_count)[:, None] == jnp.arange(tok_count, dtype=jnp.int32)[None, :]
    ).astype(jnp.bfloat16)
    picking = jnp.dot(placing, owner_map, preferred_element_type=jnp.float32).astype(jnp.bfloat16)
    outgoing = jnp.dot(picking, tokens, preferred_element_type=jnp.float32).astype(jnp.bfloat16)
    weights = route_weight.reshape(-1)
    framed = jnp.repeat(outgoing.reshape(slot_total, most_rows, model_width), shard_count, axis=0)
    projected = jnp.einsum(
        "nmd,df->nmf",
        lax.all_to_all(framed, ("node", "expert"), split_axis=0, concat_axis=0, tiled=True),
        gate_up[0],
        preferred_element_type=jnp.float32,
    )
    hidden = (jax.nn.silu(projected[..., :ffw_piece]) * projected[..., ffw_piece:]).astype(
        jnp.bfloat16
    )
    returned = lax.all_to_all(
        jnp.einsum("nmf,fd->nmd", hidden, down_proj[0], preferred_element_type=jnp.float32).astype(
            jnp.bfloat16
        ),
        ("node", "expert"),
        split_axis=0,
        concat_axis=0,
        tiled=True,
    )
    shard_range = jnp.arange(shard_count, dtype=jnp.int32)
    row_index = (pair_slot[:, None] * shard_count + shard_range[None, :]) * most_rows + ranking[
        :, None
    ]
    gathered = jnp.take(returned.reshape(devices * most_rows, model_width), row_index, axis=0)
    weighted = gathered.astype(jnp.float32) * weights[:, None, None]
    summed = jnp.sum(weighted.reshape(tok_count, top_count * shard_count, model_width), axis=1)
    return summed.astype(jnp.bfloat16)


def solution(mesh):
    placed = (
        P(("group", "node", "expert"), None),
        P(("group", "node", "expert"), None),
        P(("group", "node", "expert"), None),
        P(),
        P(("node", "expert"), None, None),
        P(("node", "expert"), None, None),
    )
    return jax.shard_map(
        shards,
        mesh=mesh,
        in_specs=placed,
        out_specs=P(("group", "node", "expert"), None),
        check_vma=False,
    )
```

profile of v0, /device:TPU:9, one launch (start us, length us, event | category | flops | bytes accessed | tf_op | source)
XLA Modules:
  0.0 381.3 jit_solution(18189669159103624035)
XLA Ops:
  0.0 0.0 copy-start
  0.0 0.8 copy.16
  0.8 0.1 eq.26
  0.9 0.7 select_reduce_fusion
  1.6 0.2 convert_reduce_fusion
  1.8 0.0 copy-done
  1.8 0.9 convolution_convert_fusion.1
  2.8 0.0 slice-start
  2.8 0.9 broadcast_in_dim.24
  3.7 0.0 slice-start.1
  3.7 165.5 %all_to_all.10 = bf16[32,16,7168]{2,1,0:T(8,128)(2,1)S(1)} all-to-all(bf16[32,16,7168]{2,1,0:T(8,128)(2,1)S(1)} %bitcast.15), channel_id=1, replica_groups=mesh['group'=1,'node'=2,'expert'=16] {'node','expert'}, dimensions={0} | all-to-all | bytes 14680064 | tf_op jit(solution)/shard_map/all_to_all | solution.py:38
  169.2 0.0 slice-done
  169.2 0.0 slice-done.1
  169.2 0.0 copy-start.1
  169.2 4.0 %fusion = f32[32,16,512]{2,1,0:T(8,128)S(1)} fusion(bf16[32,16,7168]{2,1,0:T(8,128)(2,1)S(1)} %all_to_all.10, bf16[1,7168,512]{2,1,0:T(8,128)(2,1)S(1)} %bitcast.18), kind=kOutput, calls=%fused_computation.3 | convolution fusion | flops 3758096384 | bytes 15728640 | tf_op jit(solution)/shard_map/nmd,df->nmf/dot_general | solution.py:36
  173.2 0.0 copy-done.1
  173.2 5.1 %convolution_convert_fusion = bf16[32,16,7168]{2,1,0:T(8,128)(2,1)} fusion(bf16[1,256,7168]{2,1,0:T(8,128)(2,1)S(1)} %copy-done.1, f32[32,16,512]{2,1,0:T(8,128)S(1)} %fusion), kind=kOutput, calls=%fused_computation.1 | convolution fusion | flops 1883504640 | bytes 12058624 | tf_op jit(solution)/shard_map/nmf,fd->nmd/dot_general | solution.py:46
  178.3 0.0 copy-start.2
  178.3 7.2 %all-to-all-start.1 = ((bf16[32,16,7168]{2,1,0:T(8,128)(2,1)}), bf16[32,16,7168]{2,1,0:T(8,128)(2,1)}, u32[]{:S(2)}, u32[]{:S(2)}) async-start(bf16[32,16,7168]{2,1,0:T(8,128)(2,1)} %convolution_convert_fusion), calls=%async_computation.1 | async-start | bytes 14680064 | tf_op jit(solution)/shard_map/all_to_all | solution.py:45
  185.5 0.1 compare_select_fusion
  185.6 0.1 reshape.148
  185.8 0.1 copy.17
  185.9 0.0 copy-done.2
  185.9 0.1 copy.18
  186.0 0.1 mul.69
  186.1 162.4 %all-to-all-done.1 = bf16[32,16,7168]{2,1,0:T(8,128)(2,1)} async-done(((bf16[32,16,7168]{2,1,0:T(8,128)(2,1)}), bf16[32,16,7168]{2,1,0:T(8,128)(2,1)}, u32[]{:S(2)}, u32[]{:S(2)}) %all-to-all-start.1) | async-done | bytes 7340064 | tf_op jit(solution)/shard_map/all_to_all | solution.py:45
  348.5 12.1 %gather_fusion = bf16[256,7168]{1,0:T(8,128)(2,1)} fusion(bf16[512,7168]{1,0:T(8,128)(2,1)} %bitcast.6, s32[1024]{0:T(1024)S(1)} %pad_clamp_fusion), kind=kCustom, calls=%fused_computation | custom fusion | bytes 7341056 | tf_op jit(solution)/shard_map/jit(_take)/gather | solution.py:58
  360.6 7.0 %reshape.147 = bf16[64,4,7168]{2,1,0:T(4,128)(2,1)} reshape(bf16[256,7168]{1,0:T(8,128)(2,1)} %gather_fusion) | data formatting | bytes 7340032 | tf_op jit(solution)/shard_map/jit(_take)/gather | solution.py:58
  367.6 9.9 %multiply_reduce_fusion = f32[64,7168]{1,0:T(8,128)} fusion(f32[64]{0:T(128)S(1)} %mul.69, bf16[64,4,7168]{2,1,0:T(4,128)(2,1)} %reshape.147, pred[64,4]{1,0:T(8,128)(4,1)S(1)} %copy.17), kind=kLoop, calls=%fused_computation.5 | loop fusion | flops 6881280 | bytes 5505536 | tf_op jit(solution)/shard_map/reduce_sum | solution.py:60
  377.5 1.9 reduce_sum.37
  379.4 1.9 reduce_sum.38
  (4 shorter events, 0.0 us)
Async XLA Ops:
  0.0 1.8 copy-start
  2.8 166.4 %slice-start = ((s8[7340032]{0:T(1024)(128)(4,1)}), s8[4194304]{0:T(1024)(128)(4,1)S(1)}, s32[]{:S(2)}) async-start(s8[7340032]{0:T(1024)(128)(4,1)} %bitcast.17), calls=%async_computation.2 | async-start | bytes 8388608
  3.7 165.5 %slice-start.1 = ((s8[7340032]{0:T(1024)(128)(4,1)}), s8[3145728]{0:T(1024)(128)(4,1)S(1)}, s32[]{:S(2)}) async-start(s8[7340032]{0:T(1024)(128)(4,1)} %bitcast.17), calls=%async_computation.3 | async-start | bytes 6291456
  169.2 4.0 %copy-start.1 = (bf16[1,256,7168]{2,1,0:T(8,128)(2,1)S(1)}, bf16[1,256,7168]{2,1,0:T(8,128)(2,1)}, u32[]{:S(2)}) copy-start(bf16[1,256,7168]{2,1,0:T(8,128)(2,1)} %param.11) | copy-start | bytes 11010052
  178.3 7.6 %copy-start.2 = (f32[16,4]{0,1:T(4,128)S(1)}, f32[16,4]{0,1:T(4,128)}, u32[]{:S(2)}) copy-start(f32[16,4]{0,1:T(4,128)} %param.8) | copy-start | bytes 772
  178.3 170.2 %all-to-all-start.1 = ((bf16[32,16,7168]{2,1,0:T(8,128)(2,1)}), bf16[32,16,7168]{2,1,0:T(8,128)(2,1)}, u32[]{:S(2)}, u32[]{:S(2)}) async-start(bf16[32,16,7168]{2,1,0:T(8,128)(2,1)} %convolution_convert_fusion), calls=%async_computation.1 | async-start | bytes 14680064 | tf_op jit(solution)/shard_map/all_to_all | solution.py:45
where the time goes:
time: 386 us; the launch traced here: 381 us
  blocking collectives  165 us (43%)
  waiting for transfers between devices  162 us (42%)
  local copies, waits for them, and re-layouts  23.2 us (6%)
  other arithmetic  12.8 us (3%)
  matrix products  10.1 us (3%)
  starting transfers between devices  7.21 us (2%)
    all_to_all x1, blocking collectives, shards(): lax.all_to_all(framed, ('node', 'expert'), split_axis=0, concat_axis=0, t...  165 us
    all_to_all x1, waiting for transfers between devices, shards(): lax.all_to_all(jnp.einsum('nmf,fd->nmd', hidden, down_proj[0], preferred_...  162 us
    gather x2, local copies, waits for them, and re-layouts, shards(): jnp.take(returned.reshape(devices * most_rows, model_width), row_index, a...  19.1 us
    reduce_sum x2, other arithmetic, shards(): jnp.sum(weighted.reshape(tok_count, top_count * shard_count, model_width)...  11.8 us
  transfers between devices with their start and end apart: 1, of which 1 were waited for; matrix products, arithmetic and copies ran while one was open for 0% of the time, Pallas kernels for 0%

commit v1 on v0

v1 whole, which is shorter than its diff:
```python
import functools

import jax
import jax.numpy as jnp
from jax import lax
from jax.experimental import pallas as pl
from jax.experimental.pallas import tpu as pltpu
from jax.sharding import PartitionSpec as P

MESH = pl.DeviceIdType.MESH
PARTS = 2
LANES = 128


def layer_kernel(
    grid_dims, slots,
    placement_ref, tok_ref, ids_ref, rw_ref, gu_hbm, dn_hbm, out_ref,
    gath, gu, dn, acc, part_sum, sib_in, b_in, z_in, a_in,
    w_sem, g_recv, g_send, g_asend, s_send, s_recv, b_send, b_recv, z_send, z_recv, a_send, a_recv,
):
    depth, height, breadth = grid_dims
    chips = depth * height * breadth
    plane = height * breadth
    rows, width = tok_ref.shape
    half = width // PARTS
    hidden_units = dn.shape[0]
    top = ids_ref.shape[1]
    core = lax.axis_index("node")
    chip = lax.axis_index("expert")
    z = chip // plane
    y = (chip // breadth) % height
    x = chip % breadth
    base = core * chips
    own = base + chip
    other_base = (1 - core) * chips
    slot = own // (2 * chips // slots)

    a_dims = (breadth, height)
    b_dims = (height, breadth)
    a_pos = (x, y)
    b_pos = (y, x)

    def chip_at(p, zz, aa, bb):
        yy, xx = (bb, aa) if p == 0 else (aa, bb)
        return (zz * height + yy) * breadth + xx

    def dev(node, expert):
        return {"node": node, "expert": expert}

    sibling = dev(1 - core, chip)
    up = dev(core, chip + plane)
    down = dev(core, chip - plane)
    a_dev = tuple(dev(core, chip_at(p, z, 1 - a_pos[p], b_pos[p])) for p in range(PARTS))
    b_dev = tuple(dev(core, chip_at(p, z, a_pos[p], 1 - b_pos[p])) for p in range(PARTS))
    has_up = z < depth - 1
    has_down = z > 0

    gu_copy = pltpu.make_async_copy(gu_hbm.at[0], gu, w_sem.at[0])
    dn_copy = pltpu.make_async_copy(dn_hbm.at[0], dn, w_sem.at[1])
    gu_copy.start()
    dn_copy.start()

    barrier = pltpu.get_barrier_semaphore()
    pl.semaphore_signal(barrier, inc=1, device_id=sibling, device_id_type=MESH)
    fixed = 1
    for p in range(PARTS):
        if a_dims[p] > 1:
            pl.semaphore_signal(barrier, inc=1, device_id=a_dev[p], device_id_type=MESH)
            fixed += 1

    @pl.when(has_up)
    def _():
        pl.semaphore_signal(barrier, inc=1, device_id=up, device_id_type=MESH)

    @pl.when(has_down)
    def _():
        pl.semaphore_signal(barrier, inc=1, device_id=down, device_id_type=MESH)

    lane = lax.broadcasted_iota(jnp.int32, (rows, LANES), 1)
    weight = jnp.zeros((rows, LANES), jnp.float32)
    for s in range(slots):
        here = lane == placement_ref[s]
        for k in range(top):
            named = ids_ref[:, k : k + 1] == s
            weight = weight + jnp.where(here & named, rw_ref[:, k : k + 1], 0.0)
    coarse = weight.astype(jnp.bfloat16)
    fine = (weight - coarse.astype(jnp.float32)).astype(jnp.bfloat16)
    for p, extra in ((0, coarse), (1, fine)):
        gath[p, own, :, 0:half] = tok_ref[:, p * half : (p + 1) * half]
        gath[p, own, :, half : half + LANES] = extra

    pl.semaphore_wait(barrier, fixed + has_up.astype(jnp.int32) + has_down.astype(jnp.int32))

    def g_copy(p, kind, block, to):
        return pltpu.make_async_remote_copy(
            src_ref=gath.at[p, block], dst_ref=gath.at[p, block],
            send_sem=g_send.at[p, kind, block - base], recv_sem=g_recv.at[p, block],
            device_id=to, device_id_type=MESH)

    def g_a(p):
        return pltpu.make_async_remote_copy(
            src_ref=gath.at[p, own], dst_ref=gath.at[p, own],
            send_sem=g_asend.at[p], recv_sem=g_recv.at[p, own],
            device_id=a_dev[p], device_id_type=MESH)

    def g_wait(p, block):
        pltpu.make_async_remote_copy(
            src_ref=gath.at[p, block], dst_ref=gath.at[p, block],
            send_sem=g_asend.at[p], recv_sem=g_recv.at[p, block],
            device_id=sibling, device_id_type=MESH).wait_recv()

    def g_spread(p, block, go_up, go_down):
        if go_up is not None:
            @pl.when(go_up)
            def _():
                g_copy(p, 0, block, up).start()
        if go_down is not None:
            @pl.when(go_down)
            def _():
                g_copy(p, 1, block, down).start()
        if b_dims[p] > 1:
            g_copy(p, 2, block, b_dev[p]).start()
        g_copy(p, 3, block, sibling).start()

    for p in range(PARTS):
        if a_dims[p] > 1:
            g_a(p).start()
    for p in range(PARTS):
        g_spread(p, own, has_up, has_down)
    for p in range(PARTS):
        if a_dims[p] > 1:
            block = base + chip_at(p, z, 1 - a_pos[p], b_pos[p])
            g_wait(p, block)
            g_spread(p, block, has_up, has_down)

    def g_from_b(zz):
        for p in range(PARTS):
            if b_dims[p] > 1:
                for aa in range(a_dims[p]):
                    block = base + chip_at(p, zz, aa, 1 - b_pos[p])
                    g_wait(p, block)
                    g_copy(p, 3, block, sibling).start()

    def g_hop(h, carry):
        for low in (True, False):
            zz = z - h if low else z + h
            there = zz >= 0 if low else zz < depth

            @pl.when(there)
            def _():
                for p in range(PARTS):
                    for aa in range(a_dims[p]):
                        block = base + chip_at(p, zz, aa, b_pos[p])
                        g_wait(p, block)
                        g_spread(p, block, has_up if low else None, None if low else has_down)
        for low in (True, False):
            zz = z - (h - 1) if low else z + (h - 1)
            there = (zz >= 0) if low else ((zz < depth) & (h > 1))

            @pl.when(there)
            def _():
                g_from_b(zz)
        return carry

    lax.fori_loop(1, depth, g_hop, 0)
    for zz in (z - (depth - 1), z + (depth - 1)) if depth > 1 else (z,):
        @pl.when((zz >= 0) & (zz < depth))
        def _():
            g_from_b(zz)

    def g_other(e, carry):
        for p in range(PARTS):
            g_wait(p, other_base + e)
        return carry

    lax.fori_loop(0, chips, g_other, 0)

    gu_copy.wait()
    dn_copy.wait()
    blocks = min(chips, max(1, 256 // rows))
    per_core = chips // blocks
    tile = half // (half // 512) if half % 512 == 0 else half

    def compute(first):
        count = blocks * rows

        def rows_of(p, lo, hi):
            return gath[p, pl.ds(first, blocks), :, lo:hi].reshape(count, hi - lo)

        acc[...] = jnp.dot(rows_of(0, 0, half), gu[0:half, :], preferred_element_type=jnp.float32)
        acc[...] += jnp.dot(rows_of(1, 0, half), gu[half:width, :], preferred_element_type=jnp.float32)
        gate = acc[:, 0:hidden_units]
        hidden = (gate * jax.nn.sigmoid(gate) * acc[:, hidden_units:]).astype(jnp.bfloat16)
        both = rows_of(0, half, half + LANES).astype(jnp.float32) + rows_of(1, half, half + LANES).astype(jnp.float32)
        at = lax.broadcasted_iota(jnp.int32, (count, LANES), 1)
        factor = jnp.sum(jnp.where(at == slot, both, 0.0), axis=1, keepdims=True)
        for p in range(PARTS):
            for t in range(half // tile):
                lo = t * tile
                result = jnp.dot(hidden, dn[:, p * half + lo : p * half + lo + tile], preferred_element_type=jnp.float32)
                part_sum[p, pl.ds(first, blocks), :, lo : lo + tile] = (
                    (result * factor).astype(jnp.bfloat16).reshape(blocks, rows, tile))

    def s_copy(p, zz):
        return pltpu.make_async_remote_copy(
            src_ref=part_sum.at[p, pl.ds(other_base + zz * plane, plane)],
            dst_ref=sib_in.at[p, pl.ds(zz * plane, plane)],
            send_sem=s_send.at[p, zz], recv_sem=s_recv.at[p, zz],
            device_id=sibling, device_id_type=MESH)

    def order(i):
        return jnp.where(i % 2 == 0, depth - 1 - i // 2, i // 2)

    def compute_chunk(i, carry):
        compute(jnp.where(i < per_core, other_base, base - per_core * blocks) + i * blocks)

        @pl.when(i == per_core - 1)
        def _():
            def send(j, carry2):
                for p in range(PARTS):
                    s_copy(p, order(j)).start()
                return carry2
            lax.fori_loop(0, depth, send, 0)
        return carry

    lax.fori_loop(0, 2 * per_core, compute_chunk, 0)

    def add(p, block, incoming):
        part_sum[p, block] = (
            part_sum[p, block].astype(jnp.float32) + incoming.astype(jnp.float32)).astype(jnp.bfloat16)

    def b_copy(p, zz, aa):
        return pltpu.make_async_remote_copy(
            src_ref=part_sum.at[p, base + chip_at(p, zz, aa, 1 - b_pos[p])],
            dst_ref=b_in.at[p, zz * a_dims[p] + aa],
            send_sem=b_send.at[p, zz * a_dims[p] + aa], recv_sem=b_recv.at[p, zz * a_dims[p] + aa],
            device_id=b_dev[p], device_id_type=MESH)

    def z_copy(p, aa, zz, place, to):
        return pltpu.make_async_remote_copy(
            src_ref=part_sum.at[p, base + chip_at(p, zz, aa, b_pos[p])],
            dst_ref=z_in.at[p, place * a_dims[p] + aa],
            send_sem=z_send.at[p, zz * a_dims[p] + aa], recv_sem=z_recv.at[p, place * a_dims[p] + aa],
            device_id=to, device_id_type=MESH)

    def z_take(p, aa, zz, place):
        z_copy(p, aa, zz, place, up).wait_recv()
        add(p, base + chip_at(p, zz, aa, b_pos[p]), z_in[p, place * a_dims[p] + aa])

    def from_sibling(zz):
        for p in range(PARTS):
            s_copy(p, zz).wait_recv()
        for p in range(PARTS):
            for k in range(plane):
                add(p, base + zz * plane + k, sib_in[p, zz * plane + k])
            if b_dims[p] > 1:
                for aa in range(a_dims[p]):
                    b_copy(p, zz, aa).start()

    def along_z(zz):
        for p in range(PARTS):
            for aa in range(a_dims[p]):
                if b_dims[p] > 1:
                    b_copy(p, zz, aa).wait_recv()
                    add(p, base + chip_at(p, zz, aa, b_pos[p]), b_in[p, zz * a_dims[p] + aa])

                @pl.when(zz > z)
                def _():
                    @pl.when(has_down)
                    def _():
                        z_take(p, aa, zz, zz)
                    z_copy(p, aa, zz, zz, up).start()

                @pl.when(zz < z)
                def _():
                    @pl.when(has_up)
                    def _():
                        z_take(p, aa, zz, zz)
                    z_copy(p, aa, zz, jnp.where(zz == z - 1, depth, zz), down).start()

    def back(i, carry):
        @pl.when(i < depth)
        def _():
            from_sibling(order(i))

        @pl.when(i > 0)
        def _():
            along_z(order(i - 1))
        return carry

    lax.fori_loop(0, depth + 1, back, 0)
    for aa_off in range(2):
        for p in range(PARTS):
            if a_dims[p] > 1 or aa_off == 1:
                aa = 1 - a_pos[p] if aa_off == 0 else a_pos[p]

                @pl.when(has_down)
                def _():
                    z_take(p, aa, z, z)

                @pl.when(has_up)
                def _():
                    z_take(p, aa, z, depth)

            if a_dims[p] > 1 and aa_off == 0:
                pltpu.make_async_remote_copy(
                    src_ref=part_sum.at[p, base + chip_at(p, z, aa, b_pos[p])], dst_ref=a_in.at[p],
                    send_sem=a_send.at[p], recv_sem=a_recv.at[p],
                    device_id=a_dev[p], device_id_type=MESH).start()
    for p in range(PARTS):
        total = part_sum[p, own].astype(jnp.float32)
        if a_dims[p] > 1:
            last = pltpu.make_async_remote_copy(
                src_ref=part_sum.at[p, base + chip_at(p, z, 1 - a_pos[p], b_pos[p])], dst_ref=a_in.at[p],
                send_sem=a_send.at[p], recv_sem=a_recv.at[p],
                device_id=a_dev[p], device_id_type=MESH)
            last.wait_recv()
            total = total + a_in[p].astype(jnp.float32)
            last.wait_send()
            g_a(p).wait_send()
        out_ref[:, p * half : (p + 1) * half] = total.astype(jnp.bfloat16)

    def drain(zz, carry):
        for p in range(PARTS):
            s_copy(p, zz).wait_send()
            for aa in range(a_dims[p]):
                if b_dims[p] > 1:
                    b_copy(p, zz, aa).wait_send()
                    g_copy(p, 3, base + chip_at(p, zz, aa, 1 - b_pos[p]), sibling).wait_send()
                    g_copy(p, 2, base + chip_at(p, zz, aa, b_pos[p]), b_dev[p]).wait_send()
                block = base + chip_at(p, zz, aa, b_pos[p])
                g_copy(p, 3, block, sibling).wait_send()

                @pl.when((zz <= z) & has_up)
                def _():
                    g_copy(p, 0, block, up).wait_send()

                @pl.when((zz >= z) & has_down)
                def _():
                    g_copy(p, 1, block, down).wait_send()

                @pl.when(zz != z)
                def _():
                    z_copy(p, aa, zz, zz, up).wait_send()
        return carry

    lax.fori_loop(0, depth, drain, 0)


def shards(grid_dims, tokens, copy_ids, route_weight, placement, gate_up, down_proj):
    rows, width = tokens.shape
    slots = placement.shape[0]
    depth, height, breadth = grid_dims
    chips = depth * height * breadth
    devices = 2 * chips
    half = width // PARTS
    most = max(height, breadth)
    count = min(chips, max(1, 256 // rows)) * rows
    dma = pltpu.SemaphoreType.DMA
    vmem = pl.BlockSpec(memory_space=pltpu.VMEM)
    return pl.pallas_call(
        functools.partial(layer_kernel, grid_dims, slots),
        out_shape=jax.ShapeDtypeStruct((rows, width), jnp.bfloat16),
        in_specs=[
            pl.BlockSpec(memory_space=pltpu.SMEM), vmem, vmem, vmem,
            pl.BlockSpec(memory_space=pl.ANY), pl.BlockSpec(memory_space=pl.ANY),
        ],
        out_specs=vmem,
        scratch_shapes=[
            pltpu.VMEM((PARTS, devices, rows, half + LANES), jnp.bfloat16),
            pltpu.VMEM(gate_up.shape[1:], jnp.bfloat16),
            pltpu.VMEM(down_proj.shape[1:], jnp.bfloat16),
            pltpu.VMEM((count, gate_up.shape[2]), jnp.float32),
            pltpu.VMEM((PARTS, devices, rows, half), jnp.bfloat16),
            pltpu.VMEM((PARTS, chips, rows, half), jnp.bfloat16),
            pltpu.VMEM((PARTS, depth * most if most > 1 else 1, rows, half), jnp.bfloat16),
            pltpu.VMEM((PARTS, (depth + 1) * most, rows, half), jnp.bfloat16),
            pltpu.VMEM((PARTS, rows, half), jnp.bfloat16),
            dma((2,)),
            dma((PARTS, devices)),
            dma((PARTS, 4, chips)),
            dma((PARTS,)),
            dma((PARTS, depth)),
            dma((PARTS, depth)),
            dma((PARTS, depth * most)),
            dma((PARTS, depth * most)),
            dma((PARTS, depth * most)),
            dma((PARTS, (depth + 1) * most)),
            dma((PARTS,)),
            dma((PARTS,)),
        ],
        compiler_params=pltpu.CompilerParams(
            collective_id=0, has_side_effects=True, vmem_limit_bytes=62 * 2**20),
        cost_estimate=pl.CostEstimate(
            flops=6 * devices * rows * width * down_proj.shape[1],
            bytes_accessed=2 * 3 * width * down_proj.shape[1], transcendentals=0),
    )(placement, tokens, copy_ids, route_weight, gate_up, down_proj)


def solution(mesh):
    chips = mesh.shape["expert"]
    grid_dims = (chips // 4, 2, 2) if mesh.shape["group"] == 1 and chips % 4 == 0 else (chips, 1, 1)
    placed = (
        P(("group", "node", "expert"), None),
        P(("group", "node", "expert"), None),
        P(("group", "node", "expert"), None),
        P(),
        P(("node", "expert"), None, None),
        P(("node", "expert"), None, None),
    )
    return jax.shard_map(
        functools.partial(shards, grid_dims),
        mesh=mesh,
        in_specs=placed,
        out_specs=P(("group", "node", "expert"), None),
        check_vma=False,
    )
```

time: 386 us -> 105 us (0.27)
  blocking collectives: 165 us -> 0 us
  waiting for transfers between devices: 162 us -> 0 us
  Pallas kernels: 0 us -> 99.6 us
  local copies, waits for them, and re-layouts: 23.2 us -> 4.35 us
  other arithmetic: 12.8 us -> 0 us
  matrix products: 10.1 us -> 0 us
  starting transfers between devices: 7.21 us -> 0 us
    all_to_all x1 -> x0, blocking collectives: 165 us -> none  [shards(): lax.all_to_all(framed, ('node', 'expert'), split_axis=0, concat_axis=0, t...]
    all_to_all x1 -> x0, waiting for transfers between devices: 162 us -> none  [shards(): lax.all_to_all(jnp.einsum('nmf,fd->nmd', hidden, down_proj[0], preferred_...]
    pallas_call x0 -> x1, Pallas kernels: none -> 99.6 us  [shards(): pl.pallas_call(functools.partial(layer_kernel, grid_dims, slots), out_sha...]
    gather x2 -> x0, local copies, waits for them, and re-layouts: 19.1 us -> none  [shards(): jnp.take(returned.reshape(devices * most_rows, model_width), row_index, a...]
    reduce_sum x4 -> x0, other arithmetic: 12.7 us -> none  [the longest x2 11.8 us: shards(): jnp.sum(weighted.reshape(tok_count, top_count * shard_count, model_width)...]
    dot_general x3 -> x0, matrix products: 10.1 us -> none  [the longest x1 5.15 us: shards(): jnp.einsum('nmf,fd->nmd', hidden, down_proj[0], preferred_element_type=jn...]
    all_to_all x1 -> x0, starting transfers between devices: 7.21 us -> none  [shards(): lax.all_to_all(jnp.einsum('nmf,fd->nmd', hidden, down_proj[0], preferred_...]
  transfers between devices with their start and end apart: 1 -> 0, of which waited for: 1 -> 0; matrix products, arithmetic and copies ran while one was open for 0% -> 0% of each run, Pallas kernels for 0% -> 0%
where the time goes in v1:
time: 105 us; the launch traced here: 104 us
  Pallas kernels  99.6 us (95%)
  local copies, waits for them, and re-layouts  4.35 us (4%)
    pallas_call x1, Pallas kernels, shards(): pl.pallas_call(functools.partial(layer_kernel, grid_dims, slots), out_sha...  99.6 us
    unnamed x3, local copies, waits for them, and re-layouts  4.35 us

profile of v1, /device:TPU:9, one launch (start us, length us, event | category | flops | bytes accessed | tf_op | source)
XLA Modules:
  0.0 103.9 jit_solution(273939923476966728)
XLA Ops:
  0.0 1.4 %copy.7.ids_ref = s32[16,4]{1,0:T(8,128)} copy(s32[16,4]{0,1:T(4,128)} %param.7) | data formatting | bytes 512 | tf_op args[1]
  1.4 1.4 %copy.8.rw_ref = f32[16,4]{1,0:T(8,128)} copy(f32[16,4]{0,1:T(4,128)} %param.8) | data formatting | bytes 512 | tf_op args[2]
  2.7 99.6 %shard_map.64 = bf16[16,7168]{1,0:T(8,128)(2,1)} custom-call(s32[8]{0:T(128)} %placement_ref.1, bf16[16,7168]{1,0:T(8,128)(2,1)} %tok_ref.1, s32[16,4]{1,0:T(8,128)} %copy.7.ids_ref, f32[16,4]{1,0:T(8,128)} %copy.8.rw_ref, bf16[1,7168,512]{2,1,0:T(8,128)(2,1)} %gu_hbm.1, bf16[1,256,7168]{2,1,0:T(8,128)(2,1)} %dn_hbm.1), custom_call_target="tpu_custom_call" | custom-call | flops 5637144576 | bytes 11010048 | tf_op jit(solution)/shard_map/pallas_call | solution.py:361
  102.3 1.6 %copy.10 = bf16[16,7168]{1,0:T(8,128)(2,1)} copy(bf16[16,7168]{1,0:T(8,128)(2,1)} %shard_map.64) | data formatting | bytes 458752

commit v2 on v0

v2 whole, which is shorter than its diff:
```python
import functools

import jax
import jax.numpy as jnp
from jax import lax
from jax.experimental import pallas as pl
from jax.experimental.pallas import tpu as pltpu
from jax.sharding import PartitionSpec as P

MESH = pl.DeviceIdType.MESH
PARTS = 2
LANES = 128


def layer_kernel(
    grid_dims, slots,
    placement_ref, tok_ref, ids_ref, rw_ref, gu_hbm, dn_hbm, out_ref,
    gath, gu, dn, acc, hid, fac, part_sum, sib_in, b_in, z_in, a_in, fin, f_in,
    w_sem, g_recv, g_send, gz_send, g_isend, s_send, s_recv, b_send, b_recv, z_send, z_recv,
    a_send, a_recv, f_sem,
):
    depth, side = grid_dims
    plane = side * side
    chips = depth * plane
    rows, width = tok_ref.shape
    half = width // PARTS
    hidden_units = hid.shape[1]
    top = ids_ref.shape[1]
    core = lax.axis_index("node")
    chip = lax.axis_index("expert")
    z = chip // plane
    y = (chip // side) % side
    x = chip % side
    own = core * chips + chip
    mate = (1 - core) * chips + chip
    slot = own // (2 * chips // slots)

    first = core == 0
    a_step = jnp.where(first, 1, side)
    b_step = jnp.where(first, side, 1)
    a_pos = jnp.where(first, x, y)
    b_pos = jnp.where(first, y, x)

    def chip_at(zz, aa, bb):
        return zz * plane + aa * a_step + bb * b_step

    def dev(node, expert):
        return {"node": node, "expert": expert}

    sibling = dev(1 - core, chip)
    a_dev = dev(core, chip_at(z, 1 - a_pos, b_pos))
    b_dev = dev(core, chip_at(z, a_pos, 1 - b_pos))

    w_copies = [pltpu.make_async_copy(gu_hbm.at[0], gu, w_sem.at[0])] + [
        pltpu.make_async_copy(dn_hbm.at[0, :, pl.ds(p * half, half)], dn.at[p], w_sem.at[1 + p])
        for p in range(PARTS)]
    for copy in w_copies:
        copy.start()

    barrier = pltpu.get_barrier_semaphore()
    near = [sibling] + ([a_dev, b_dev] if side > 1 else [])
    for to in near:
        pl.semaphore_signal(barrier, inc=1, device_id=to, device_id_type=MESH)

    def greet(h, carry):
        zz = lax.rem(z + h, depth)
        pl.semaphore_signal(barrier, inc=1, device_id=dev(core, chip_at(zz, a_pos, b_pos)), device_id_type=MESH)
        return carry

    lax.fori_loop(1, depth, greet, 0)

    lane = lax.broadcasted_iota(jnp.int32, (rows, LANES), 1)
    weight = jnp.zeros((rows, LANES), jnp.float32)
    for s in range(slots):
        here = lane == placement_ref[s]
        for k in range(top):
            named = ids_ref[:, k : k + 1] == s
            weight = weight + jnp.where(here & named, rw_ref[:, k : k + 1], 0.0)
    coarse = weight.astype(jnp.bfloat16)
    fine = (weight - coarse.astype(jnp.float32)).astype(jnp.bfloat16)
    for p, extra in ((0, coarse), (1, fine)):
        gath[p, own, :, 0:half] = tok_ref[:, p * half : (p + 1) * half]
        gath[p, own, :, half : half + LANES] = extra

    pl.semaphore_wait(barrier, len(near) + depth - 1)

    def remote(src, dst, send, recv, to):
        return pltpu.make_async_remote_copy(
            src_ref=src, dst_ref=dst, send_sem=send, recv_sem=recv, device_id=to, device_id_type=MESH)

    def g_copy(sem, k, ch, to):
        block = k * chips + ch
        return remote(gath.at[core, block], gath.at[core, block], sem, g_recv.at[core, block], to)

    def g_z(k, zz):
        return g_copy(gz_send.at[k, zz], k, chip, dev(core, chip_at(zz, a_pos, b_pos)))

    def g_to(kind, k, ch):
        return g_copy(g_send.at[kind, k * chips + ch], k, ch, (a_dev, b_dev, sibling)[kind])

    def g_mate(p):
        return remote(gath.at[p, own], gath.at[p, own], g_isend.at[p], g_recv.at[p, own], sibling)

    def g_wait(p, block):
        remote(gath.at[p, block], gath.at[p, block], g_isend.at[p], g_recv.at[p, block], sibling).wait_recv()

    def planes(h, act):
        @pl.when(z - h >= 0)
        def _():
            act(z - h)

        @pl.when((z + h < depth) & (h != 0))
        def _():
            act(z + h)

    def g_begin(k):
        @pl.when(core != k)
        def _():
            g_wait(core, mate)

        def one(h, carry):
            planes(h, lambda zz: g_z(k, zz).start())
            return carry

        if side > 1:
            g_to(1, k, chip).start()
            g_to(0, k, chip).start()
        lax.fori_loop(1, depth, one, 0)

    def g_steps(k, lo, hi):
        def from_z(zz):
            ch = chip_at(zz, a_pos, b_pos)
            g_wait(core, k * chips + ch)
            if side > 1:
                g_to(0, k, ch).start()
                g_to(1, k, ch).start()
            g_to(2, k, ch).start()

        def from_a(zz):
            ch = chip_at(zz, 1 - a_pos, b_pos)
            g_wait(core, k * chips + ch)
            g_to(1, k, ch).start()
            g_to(2, k, ch).start()

        def from_b(zz):
            for aa in range(side):
                ch = chip_at(zz, aa, 1 - b_pos)
                g_wait(core, k * chips + ch)
                g_to(2, k, ch).start()

        def one(h, carry):
            @pl.when((h >= 1) & (h < depth))
            def _():
                planes(h, from_z)
            if side > 1:
                @pl.when((h >= 1) & (h <= depth))
                def _():
                    planes(h - 1, from_a)

                @pl.when(h >= 2)
                def _():
                    planes(h - 2, from_b)
            return carry

        lax.fori_loop(lo, hi, one, 0)

    def g_end(k):
        def g_other(e, carry):
            @pl.when((e != chip) | (core != k))
            def _():
                g_wait(1 - core, k * chips + e)
            return carry

        lax.fori_loop(0, chips, g_other, 0)

    blocks = min(chips, max(1, 256 // rows))
    count = blocks * rows
    tile = 512 if half % 512 == 0 else half

    def gate_up(k):
        def one(i, carry):
            at = k * chips + i * blocks
            here = pl.ds(pl.multiple_of(i * count, count), count)

            def rows_of(p, lo, hi):
                return gath[p, pl.ds(at, blocks), :, lo:hi].reshape(count, hi - lo)

            acc[...] = jnp.dot(rows_of(0, 0, half), gu[0:half, :], preferred_element_type=jnp.float32)
            acc[...] += jnp.dot(rows_of(1, 0, half), gu[half:width, :], preferred_element_type=jnp.float32)
            gate = acc[:, 0:hidden_units]
            hid[here, :] = (gate * jax.nn.sigmoid(gate) * acc[:, hidden_units:]).astype(jnp.bfloat16)
            both = rows_of(0, half, half + LANES).astype(jnp.float32) + rows_of(1, half, half + LANES).astype(jnp.float32)
            lanes = lax.broadcasted_iota(jnp.int32, (count, LANES), 1)
            factor = jnp.sum(jnp.where(lanes == slot, both, 0.0), axis=1, keepdims=True)
            fac[here, :] = jnp.broadcast_to(factor, (count, LANES))
            return carry

        lax.fori_loop(0, chips // blocks, one, 0)

    def down_proj(k, p):
        def one(i, carry):
            at = k * chips + i * blocks
            here = pl.ds(pl.multiple_of(i * count, count), count)
            hidden = hid[here, :]
            factor = fac[here, 0:1]
            for t in range(half // tile):
                lo = t * tile
                result = jnp.dot(hidden, dn[p, :, lo : lo + tile], preferred_element_type=jnp.float32)
                part_sum[p, pl.ds(at, blocks), :, lo : lo + tile] = (
                    (result * factor).astype(jnp.bfloat16).reshape(blocks, rows, tile))
            return carry

        lax.fori_loop(0, chips // blocks, one, 0)

    def order(i):
        return jnp.where(i % 2 == 0, depth - 1 - i // 2, i // 2)

    def s_copy(k, zz):
        here = pl.ds(k * chips + zz * plane, plane)
        return remote(part_sum.at[1 - core, here], sib_in.at[here], s_send.at[k, zz], s_recv.at[k, zz], sibling)

    def to_sibling(k):
        def one(i, carry):
            s_copy(k, order(i)).start()
            return carry
        lax.fori_loop(0, depth, one, 0)

    def add(block, incoming):
        part_sum[core, block] = (
            part_sum[core, block].astype(jnp.float32) + incoming.astype(jnp.float32)).astype(jnp.bfloat16)

    def a_copy(k, zz):
        return remote(part_sum.at[core, k * chips + chip_at(zz, 1 - a_pos, b_pos)], a_in.at[k, zz],
                      a_send.at[k, zz], a_recv.at[k, zz], a_dev)

    def b_copy(k, zz, near_a):
        aa = a_pos if near_a else 1 - a_pos
        place = 2 * zz + (1 if near_a else 0)
        return remote(part_sum.at[core, k * chips + chip_at(zz, aa, 1 - b_pos)], b_in.at[k, place],
                      b_send.at[k, place], b_recv.at[k, place], b_dev)

    def z_copy(k, zz):
        return remote(part_sum.at[core, k * chips + chip_at(zz, a_pos, b_pos)], z_in.at[k, z],
                      z_send.at[k, zz], z_recv.at[k, z], dev(core, chip_at(zz, a_pos, b_pos)))

    def z_wait(k, zz):
        remote(z_in.at[k, zz], z_in.at[k, zz], z_send.at[k, zz], z_recv.at[k, zz], sibling).wait_recv()

    def from_sibling(k):
        def one(i, carry):
            zz = order(i)
            s_copy(k, zz).wait_recv()
            for j in range(plane):
                block = k * chips + zz * plane + j
                add(block, sib_in[block])
            if side > 1:
                b_copy(k, zz, False).start()
                b_copy(k, zz, True).start()
            return carry
        lax.fori_loop(0, depth, one, 0)

    def along_b(k, lo, hi):
        def one(i, carry):
            zz = order(i)
            for near_a in (False, True):
                b_copy(k, zz, near_a).wait_recv()
                aa = a_pos if near_a else 1 - a_pos
                add(k * chips + chip_at(zz, aa, b_pos), b_in[k, 2 * zz + (1 if near_a else 0)])
                if not near_a:
                    a_copy(k, zz).start()
            return carry
        if side > 1:
            lax.fori_loop(lo, hi, one, 0)

    def along_a(k, lo, hi):
        def one(i, carry):
            zz = order(i)
            if side > 1:
                a_copy(k, zz).wait_recv()
                add(k * chips + chip_at(zz, a_pos, b_pos), a_in[k, zz])

            @pl.when(zz != z)
            def _():
                z_copy(k, zz).start()
            return carry
        lax.fori_loop(lo, hi, one, 0)

    def along_both(k):
        def one(i, carry):
            @pl.when(i < depth)
            def _():
                along_b(k, i, i + 1)

            @pl.when(i > 0)
            def _():
                along_a(k, i - 1, i)
            return carry
        lax.fori_loop(0, depth + 1, one, 0)

    def f_copy():
        return remote(fin.at[1 - core], f_in, f_sem.at[0], f_sem.at[1], sibling)

    def finish(k):
        def one(h, total):
            def take(zz, total):
                z_wait(k, zz)
                return total + z_in[k, zz].astype(jnp.float32)
            zz = lax.rem(z + h, depth)
            return take(zz, total)
        total = lax.fori_loop(1, depth, one, part_sum[core, k * chips + chip].astype(jnp.float32))
        fin[k] = total.astype(jnp.bfloat16)

        @pl.when(core != k)
        def _():
            f_copy().start()

    for p in range(PARTS):
        g_mate(p).start()
    g_begin(0)
    g_steps(0, 1, 2)
    g_begin(1)
    g_steps(0, 2, depth + 2)
    g_steps(1, 1, 3)
    g_end(0)
    for copy in w_copies:
        copy.wait()
    gate_up(0)
    g_steps(1, 3, depth + 1)
    down_proj(0, 1 - core)
    to_sibling(0)
    down_proj(0, core)
    g_steps(1, depth + 1, depth + 2)
    from_sibling(0)
    g_end(1)
    gate_up(1)
    down_proj(1, 1 - core)
    to_sibling(1)
    along_both(0)
    down_proj(1, core)
    from_sibling(1)
    along_both(1)
    finish(0)
    finish(1)
    f_copy().wait_recv()
    for c in range(PARTS):
        @pl.when(core == c)
        def _():
            out_ref[:, c * half : (c + 1) * half] = fin[c]
            out_ref[:, (1 - c) * half : (2 - c) * half] = f_in[...]

    f_copy().wait_send()
    for p in range(PARTS):
        g_mate(p).wait_send()
    for k in range(2):
        def drain(zz, carry):
            s_copy(k, zz).wait_send()
            ch = chip_at(zz, a_pos, b_pos)
            if side > 1:
                a_copy(k, zz).wait_send()
                g_to(0, k, ch).wait_send()
                for aa in range(side):
                    b_copy(k, zz, aa == 1).wait_send()
                    g_to(1, k, chip_at(zz, aa, b_pos)).wait_send()
                    g_to(2, k, chip_at(zz, aa, 1 - b_pos)).wait_send()
                g_to(2, k, chip_at(zz, 1 - a_pos, b_pos)).wait_send()

            @pl.when(zz != z)
            def _():
                g_to(2, k, ch).wait_send()
                g_z(k, zz).wait_send()
                z_copy(k, zz).wait_send()
            return carry

        lax.fori_loop(0, depth, drain, 0)


def shards(grid_dims, tokens, copy_ids, route_weight, placement, gate_up, down_proj):
    rows, width = tokens.shape
    slots = placement.shape[0]
    depth, side = grid_dims
    chips = depth * side * side
    devices = 2 * chips
    half = width // PARTS
    hidden_units = down_proj.shape[1]
    count = min(chips, max(1, 256 // rows)) * rows
    dma = pltpu.SemaphoreType.DMA
    vmem = pl.BlockSpec(memory_space=pltpu.VMEM)
    return pl.pallas_call(
        functools.partial(layer_kernel, grid_dims, slots),
        out_shape=jax.ShapeDtypeStruct((rows, width), jnp.bfloat16),
        in_specs=[
            pl.BlockSpec(memory_space=pltpu.SMEM), vmem, vmem, vmem,
            pl.BlockSpec(memory_space=pl.ANY), pl.BlockSpec(memory_space=pl.ANY),
        ],
        out_specs=vmem,
        scratch_shapes=[
            pltpu.VMEM((PARTS, devices, rows, half + LANES), jnp.bfloat16),
            pltpu.VMEM(gate_up.shape[1:], jnp.bfloat16),
            pltpu.VMEM((PARTS, hidden_units, half), jnp.bfloat16),
            pltpu.VMEM((count, gate_up.shape[2]), jnp.float32),
            pltpu.VMEM((chips * rows, hidden_units), jnp.bfloat16),
            pltpu.VMEM((chips * rows, LANES), jnp.float32),
            pltpu.VMEM((PARTS, devices, rows, half), jnp.bfloat16),
            pltpu.VMEM((devices, rows, half), jnp.bfloat16),
            pltpu.VMEM((2, 2 * depth if side > 1 else 1, rows, half), jnp.bfloat16),
            pltpu.VMEM((2, depth, rows, half), jnp.bfloat16),
            pltpu.VMEM((2, depth if side > 1 else 1, rows, half), jnp.bfloat16),
            pltpu.VMEM((2, rows, half), jnp.bfloat16),
            pltpu.VMEM((rows, half), jnp.bfloat16),
            dma((1 + PARTS,)),
            dma((PARTS, devices)),
            dma((3, devices)),
            dma((2, depth)),
            dma((PARTS,)),
            dma((2, depth)),
            dma((2, depth)),
            dma((2, 2 * depth)),
            dma((2, 2 * depth)),
            dma((2, depth)),
            dma((2, depth)),
            dma((2, depth)),
            dma((2, depth)),
            dma((2,)),
        ],
        compiler_params=pltpu.CompilerParams(
            collective_id=0, has_side_effects=True, vmem_limit_bytes=62 * 2**20),
        cost_estimate=pl.CostEstimate(
            flops=6 * devices * rows * width * down_proj.shape[1],
            bytes_accessed=2 * 3 * width * down_proj.shape[1], transcendentals=0),
    )(placement, tokens, copy_ids, route_weight, gate_up, down_proj)


def solution(mesh):
    chips = mesh.shape["expert"]
    grid_dims = (chips // 4, 2) if mesh.shape["group"] == 1 and chips % 4 == 0 else (chips, 1)
    placed = (
        P(("group", "node", "expert"), None),
        P(("group", "node", "expert"), None),
        P(("group", "node", "expert"), None),
        P(),
        P(("node", "expert"), None, None),
        P(("node", "expert"), None, None),
    )
    return jax.shard_map(
        functools.partial(shards, grid_dims),
        mesh=mesh,
        in_specs=placed,
        out_specs=P(("group", "node", "expert"), None),
        check_vma=False,
    )
```

time: 386 us -> 100 us (0.26); the launches traced: 381 us -> 100 us
  blocking collectives: 165 us -> 0 us
  waiting for transfers between devices: 162 us -> 0 us
  Pallas kernels: 0 us -> 95.9 us
  local copies, waits for them, and re-layouts: 23.2 us -> 4.35 us
  other arithmetic: 12.8 us -> 0 us
  matrix products: 10.1 us -> 0 us
  starting transfers between devices: 7.21 us -> 0 us
    all_to_all x1 -> x0, blocking collectives: 165 us -> none  [shards(): lax.all_to_all(framed, ('node', 'expert'), split_axis=0, concat_axis=0, t...]
    all_to_all x1 -> x0, waiting for transfers between devices: 162 us -> none  [shards(): lax.all_to_all(jnp.einsum('nmf,fd->nmd', hidden, down_proj[0], preferred_...]
    pallas_call x0 -> x1, Pallas kernels: none -> 95.9 us  [shards(): pl.pallas_call(functools.partial(layer_kernel, grid_dims, slots), out_sha...]
    gather x2 -> x0, local copies, waits for them, and re-layouts: 19.1 us -> none  [shards(): jnp.take(returned.reshape(devices * most_rows, model_width), row_index, a...]
    reduce_sum x4 -> x0, other arithmetic: 12.7 us -> none  [the longest x2 11.8 us: shards(): jnp.sum(weighted.reshape(tok_count, top_count * shard_count, model_width)...]
    dot_general x3 -> x0, matrix products: 10.1 us -> none  [the longest x1 5.15 us: shards(): jnp.einsum('nmf,fd->nmd', hidden, down_proj[0], preferred_element_type=jn...]
    all_to_all x1 -> x0, starting transfers between devices: 7.21 us -> none  [shards(): lax.all_to_all(jnp.einsum('nmf,fd->nmd', hidden, down_proj[0], preferred_...]
  transfers between devices with their start and end apart: 1 -> 0, of which waited for: 1 -> 0; matrix products, arithmetic and copies ran while one was open for 0% -> 0% of each run, Pallas kernels for 0% -> 0%
where the time goes in v2:
time: 100 us
  Pallas kernels  95.9 us (96%)
  local copies, waits for them, and re-layouts  4.35 us (4%)
    pallas_call x1, Pallas kernels, shards(): pl.pallas_call(functools.partial(layer_kernel, grid_dims, slots), out_sha...  95.9 us
    unnamed x3, local copies, waits for them, and re-layouts  4.35 us

profile of v2, /device:TPU:9, one launch (start us, length us, event | category | flops | bytes accessed | tf_op | source)
XLA Modules:
  0.0 100.2 jit_solution(14945432567124670328)
XLA Ops:
  0.0 1.4 %copy.7.ids_ref = s32[16,4]{1,0:T(8,128)} copy(s32[16,4]{0,1:T(4,128)} %param.7) | data formatting | bytes 512 | tf_op args[1]
  1.4 1.4 %copy.8.rw_ref = f32[16,4]{1,0:T(8,128)} copy(f32[16,4]{0,1:T(4,128)} %param.8) | data formatting | bytes 512 | tf_op args[2]
  2.7 95.9 %shard_map.64 = bf16[16,7168]{1,0:T(8,128)(2,1)} custom-call(s32[8]{0:T(128)} %placement_ref.1, bf16[16,7168]{1,0:T(8,128)(2,1)} %tok_ref.1, s32[16,4]{1,0:T(8,128)} %copy.7.ids_ref, f32[16,4]{1,0:T(8,128)} %copy.8.rw_ref, bf16[1,7168,512]{2,1,0:T(8,128)(2,1)} %gu_hbm.1, bf16[1,256,7168]{2,1,0:T(8,128)(2,1)} %dn_hbm.1), custom_call_target="tpu_custom_call" | custom-call | flops 5637144576 | bytes 11010048 | tf_op jit(solution)/shard_map/pallas_call | solution.py:388
  98.6 1.6 %copy.10 = bf16[16,7168]{1,0:T(8,128)(2,1)} copy(bf16[16,7168]{1,0:T(8,128)(2,1)} %shard_map.64) | data formatting | bytes 458752

commit v3 on v2

--- a/solution.py
+++ b/solution.py
@@ -319,23 +319,29 @@
     g_begin(0)
     g_steps(0, 1, 2)
     g_begin(1)
-    g_steps(0, 2, depth + 2)
-    g_steps(1, 1, 3)
+    g_steps(0, 2, depth + 1)
+    g_steps(1, 1, 2)
+    g_steps(0, depth + 1, depth + 2)
+    g_steps(1, 2, 3)
     g_end(0)
     for copy in w_copies:
         copy.wait()
+
     gate_up(0)
-    g_steps(1, 3, depth + 1)
+    g_steps(1, 3, depth)
     down_proj(0, 1 - core)
     to_sibling(0)
+    g_steps(1, depth, depth + 1)
     down_proj(0, core)
+    from_sibling(0)
     g_steps(1, depth + 1, depth + 2)
-    from_sibling(0)
+    along_b(0, 0, depth // 2)
     g_end(1)
     gate_up(1)
+    along_b(0, depth // 2, depth)
     down_proj(1, 1 - core)
     to_sibling(1)
-    along_both(0)
+    along_a(0, 0, depth)
     down_proj(1, core)
     from_sibling(1)
     along_both(1)

time: 100 us -> 96.2 us (0.962)
  Pallas kernels: 95.9 us -> 91.6 us
    pallas_call x1, Pallas kernels: 95.9 us -> 91.6 us  [shards(): pl.pallas_call(functools.partial(layer_kernel, grid_dims, slots), out_sha...]
where the time goes in v3:
time: 96.2 us; the launch traced here: 96 us
  Pallas kernels  91.6 us (95%)
  local copies, waits for them, and re-layouts  4.35 us (5%)
    pallas_call x1, Pallas kernels, shards(): pl.pallas_call(functools.partial(layer_kernel, grid_dims, slots), out_sha...  91.6 us
    unnamed x3, local copies, waits for them, and re-layouts  4.35 us

profile of v3, /device:TPU:9, one launch (start us, length us, event | category | flops | bytes accessed | tf_op | source)
XLA Modules:
  0.0 96.0 jit_solution(7642895236276897840)
XLA Ops:
  0.0 1.4 %copy.7.ids_ref = s32[16,4]{1,0:T(8,128)} copy(s32[16,4]{0,1:T(4,128)} %param.7) | data formatting | bytes 512 | tf_op args[1]
  1.4 1.4 %copy.8.rw_ref = f32[16,4]{1,0:T(8,128)} copy(f32[16,4]{0,1:T(4,128)} %param.8) | data formatting | bytes 512 | tf_op args[2]
  2.7 91.6 %shard_map.64 = bf16[16,7168]{1,0:T(8,128)(2,1)} custom-call(s32[8]{0:T(128)} %placement_ref.1, bf16[16,7168]{1,0:T(8,128)(2,1)} %tok_ref.1, s32[16,4]{1,0:T(8,128)} %copy.7.ids_ref, f32[16,4]{1,0:T(8,128)} %copy.8.rw_ref, bf16[1,7168,512]{2,1,0:T(8,128)(2,1)} %gu_hbm.1, bf16[1,256,7168]{2,1,0:T(8,128)(2,1)} %dn_hbm.1), custom_call_target="tpu_custom_call" | custom-call | flops 5637144576 | bytes 11010048 | tf_op jit(solution)/shard_map/pallas_call | solution.py:394
  94.4 1.6 %copy.10 = bf16[16,7168]{1,0:T(8,128)(2,1)} copy(bf16[16,7168]{1,0:T(8,128)(2,1)} %shard_map.64) | data formatting | bytes 458752
